TPU v7x, 512 devices: a whole 4x4x16 slice. The times are simulated.
512 devices in a mesh: img: 32 (over z, core), orb: 16 (over y, x).
Axes of the slice: x: 4, y: 4, z: 16, core: 2. Of those that a mesh axis runs over, the one named last changes fastest.
Arguments:
- green_k: float32 [64, 8, 2, 256, 256], P('img', None, None, 'orb'), may hold values from -48 to 48
- band_of_image: int32 [64], P('img'), may hold values from 0 to 31
- fit_tensor: bfloat16 [32, 2048, 256], P(None, 'orb'), may hold values from -0.125 to 0.125
Outputs:
- sigma: float32 [64, 8, 256, 256], P('img', None, 'orb')
All inputs are finite; a program needn't handle non-finite values.
Results may differ from a plain program's by a relative error of at most 0.0041.
Values may be sent and summed in bfloat16 or wider, within the bound.
No kernel may reach another device: no remote copies, remote signals or barrier semaphores. Data moves between devices by JAX's collectives and lax.ppermute only.
A program may use at most 64 MiB of HBM per device.

v0:
```python
import math

import jax
import jax.numpy as jnp
from jax import lax
from jax.sharding import PartitionSpec as P


def mesh_phase(count, depth):
    wide = min(8, count // depth)
    tall = count // (depth * wide)
    steps = jnp.arange(count, dtype=jnp.int32)
    first = steps // (tall * depth)
    second = steps // depth % tall
    third = steps % depth
    frac = (first[:, None] * first[None, :] % wide).astype(jnp.float32) / float(wide)
    frac = frac + (second[:, None] * second[None, :] % tall).astype(jnp.float32) / float(tall)
    frac = frac + (third[:, None] * third[None, :] % depth).astype(jnp.float32) / float(depth)
    return frac * (2.0 * math.pi)


def per_device(green_k, band_of_image, fit_tensor):
    depth = green_k.shape[0]
    block = lax.all_to_all(green_k, "img", split_axis=4, concat_axis=0, tiled=True)
    count = block.shape[0]
    times_here = block.shape[1]
    rows = block.shape[3]
    cols = block.shape[4]
    phase = mesh_phase(count, depth)
    real_part = block[:, :, 0].reshape(count, -1)
    imag_part = block[:, :, 1].reshape(count, -1)
    summed = jnp.dot(jnp.cos(phase), real_part, precision=lax.Precision.HIGHEST) - jnp.dot(
        jnp.sin(phase), imag_part, precision=lax.Precision.HIGHEST
    )
    summed = (summed / count).reshape(count, times_here, rows, cols)
    images = lax.all_to_all(summed, "img", split_axis=0, concat_axis=3, tiled=True)
    blocks = jnp.take(fit_tensor, band_of_image, axis=0)
    piece = lax.all_gather(blocks, "orb", axis=1, tiled=True)
    integral = jnp.einsum("sqi,sqj->sij", piece, piece, preferred_element_type=jnp.float32)
    integral = integral.astype(jnp.bfloat16)
    green_low = images.astype(jnp.bfloat16)
    left = jnp.einsum("rtij,rjk->rtik", green_low, integral, preferred_element_type=jnp.float32)
    return left * images[:, ::-1]


def solution(mesh):
    return jax.shard_map(
        per_device,
        mesh=mesh,
        in_specs=(P("img", None, None, "orb", None), P("img"), P(None, "orb", None)),
        out_specs=P("img", None, "orb", None),
        check_vma=False,
    )
```

profile of v0, /device:TPU:1, one launch (start us, length us, event | category | flops | bytes accessed | tf_op | source)
XLA Modules:
  0.0 140.3 jit_solution(16726938893596196095)
XLA Ops:
  6.5 0.8 compare_select_fusion
  7.3 0.7 compare_and_fusion
  8.1 0.6 gather_fusion
  8.7 0.7 broadcast_select_fusion
  9.5 5.3 %copy.35 = f32[2,8,2,16,256]{3,1,2,0,4:T(8,128)} copy(f32[2,8,2,16,256]{4,3,2,1,0:T(8,128)} %param.3) | data formatting | bytes 1048576 | tf_op args[0]
  14.7 4.2 %reshape.107 = f32[32,1,4096]{2,1,0:T(1,128)} reshape(f32[256,2,2,8,16]{4,3,2,1,0:T(8,128)} %bitcast.27) | data formatting | bytes 1048576
  18.9 16.8 %all-to-all-start = ((f32[32,1,4096]{2,1,0:T(1,128)}), f32[32,1,4096]{2,1,0:T(1,128)S(1)}, u32[]{:S(2)}, u32[]{:S(2)}) async-start(f32[32,1,4096]{2,1,0:T(1,128)} %reshape.107), calls=%async_computation | async-start | bytes 1048576 | tf_op jit(solution)/shard_map/all_to_all | solution.py:24
  35.7 33.5 %all-to-all-done = f32[32,1,4096]{2,1,0:T(1,128)S(1)} async-done(((f32[32,1,4096]{2,1,0:T(1,128)}), f32[32,1,4096]{2,1,0:T(1,128)S(1)}, u32[]{:S(2)}, u32[]{:S(2)}) %all-to-all-start) | async-done | bytes 524320 | tf_op jit(solution)/shard_map/all_to_all | solution.py:24
  69.7 1.9 %reduce = f32[32,4096]{1,0:T(8,128)S(1)} reduce(f32[32,1,4096]{2,1,0:T(1,128)S(1)} %all-to-all-done, f32[]{:T(128)} %broadcast.226), dimensions={1}, to_apply=%all_to_all.26.reduce_sub_computation | reduce | bytes 1048580 | tf_op jit(solution)/shard_map/all_to_all | solution.py:24
  71.6 2.8 %reshape.108 = f32[256,2,2,8,16]{4,3,2,1,0:T(8,128)} reshape(f32[32,4096]{1,0:T(8,128)S(1)} %reduce) | data formatting | bytes 1048576
  74.4 6.0 %copy.37 = f32[32,2,8,2,16,8]{4,5,3,2,1,0:T(8,128)S(1)} copy(f32[32,2,8,2,16,8]{4,2,3,1,5,0:T(8,128)} %bitcast.29) | data formatting | bytes 1048576 | tf_op jit(solution)/shard_map/all_to_all | solution.py:24
  80.3 2.5 %fusion.43 = (f32[64,8,1,16,8]{3,4,2,1,0:T(8,128)}, f32[64,8,1,16,8]{3,4,2,1,0:T(8,128)}) fusion(f32[64,8,2,16,8]{3,4,2,1,0:T(8,128)S(1)} %bitcast.28), kind=kLoop, calls=%fused_computation.76 | loop fusion | bytes 1048576 | tf_op jit(solution)/shard_map/slice | solution.py:31
  82.9 2.7 %copy.38 = f32[64,8,1,16,8]{0,4,3,1,2:T(8,128)S(1)} copy(f32[64,8,1,16,8]{3,4,2,1,0:T(8,128)} %get-tuple-element.6) | data formatting | bytes 524288 | tf_op jit(solution)/shard_map/slice | solution.py:30
  85.6 2.7 %copy.39 = f32[64,8,1,16,8]{0,4,3,1,2:T(8,128)S(1)} copy(f32[64,8,1,16,8]{3,4,2,1,0:T(8,128)} %get-tuple-element.5) | data formatting | bytes 524288 | tf_op jit(solution)/shard_map/slice | solution.py:31
  88.3 0.9 fusion.16
  89.1 0.9 fusion
  90.2 2.9 %copy.41 = f32[64,8,16,8]{2,3,1,0:T(8,128)} copy(f32[64,8,16,8]{0,3,2,1:T(8,128)S(1)} %bitcast.35) | data formatting | bytes 524288 | tf_op jit(solution)/shard_map/reshape | solution.py:35
  93.1 2.4 %reshape.109 = f32[32,1,2048]{2,1,0:T(1,128)S(1)} reshape(f32[64,8,8,16]{3,2,1,0:T(8,128)} %bitcast.30) | data formatting | bytes 524288
  95.5 25.3 %all_to_all.36 = f32[32,1,2048]{2,1,0:T(1,128)S(1)} all-to-all(f32[32,1,2048]{2,1,0:T(1,128)S(1)} %reshape.109), channel_id=1, replica_groups=mesh['img'=32,'orb'=16] {'img'}, dimensions={0} | all-to-all | bytes 524288 | tf_op jit(solution)/shard_map/all_to_all | solution.py:36
  120.9 1.2 reduce.1
  122.1 2.1 %reshape.110 = f32[64,8,8,16]{3,2,1,0:T(8,128)} reshape(f32[32,2048]{1,0:T(8,128)S(1)} %reduce.1) | data formatting | bytes 524288
  124.2 3.1 %copy.50 = f32[2,8,16,32,8]{2,4,3,1,0:T(8,128)} copy(f32[2,8,16,32,8]{2,4,1,0,3:T(8,128)} %bitcast.31) | data formatting | bytes 524288 | tf_op jit(solution)/shard_map/all_to_all | solution.py:36
  127.3 2.2 %copy.43 = f32[2,8,16,256]{3,2,1,0:T(8,128)S(1)} copy(f32[2,8,16,256]{2,3,1,0:T(8,128)} %bitcast.32) | data formatting | bytes 524288 | tf_op jit(solution)/shard_map/all_to_all | solution.py:36
  129.5 3.9 %convolution_multiply_fusion = f32[2,8,16,256]{3,2,1,0:T(8,128)} fusion(f32[2,8,16,256]{3,2,1,0:T(8,128)S(1)} %rev.3, bf16[2,2048,256]{2,1,0:T(8,128)(2,1)} %all-gather.2.cloned.1.call-done, f32[2,8,16,256]{3,2,1,0:T(8,128)S(1)} %copy.43), kind=kOutput, calls=%fused_computation.3 | convolution fusion | flops 570687488 | bytes 2883584 | tf_op jit(solution)/shard_map/rtij,rjk->rtik/dot_general | solution.py:42
  (11 shorter events, 0.9 us)
Async XLA Ops:
  6.5 1.6 %copy-start = (bf16[32,128,256]{2,1,0:T(8,128)(2,1)S(1)}, bf16[32,128,256]{2,1,0:T(8,128)(2,1)}, u32[]{:S(2)}) copy-start(bf16[32,128,256]{2,1,0:T(8,128)(2,1)} %param.5) | copy-start | bytes 6291460
  6.5 123.0 %all-gather.2.cloned.1.call-start = ((), (), s32[]{:S(2)}) async-start(), calls=%async_computation.2 | async-start | bytes 2228224 | tf_op jit(solution)/shard_map/all_gather | solution.py:38
  18.9 50.3 %all-to-all-start = ((f32[32,1,4096]{2,1,0:T(1,128)}), f32[32,1,4096]{2,1,0:T(1,128)S(1)}, u32[]{:S(2)}, u32[]{:S(2)}) async-start(f32[32,1,4096]{2,1,0:T(1,128)} %reshape.107), calls=%async_computation | async-start | bytes 1048576 | tf_op jit(solution)/shard_map/all_to_all | solution.py:24
Sparse Core Ops, SparseCore 0:
  10.4 64.6 all-gather.1
where the time goes:
time: 141 us; the launch traced here: 140 us
  local copies, waits for them, and re-layouts  40.1 us (28%)
  waiting for transfers between devices  33.5 us (24%)
  blocking collectives  25.3 us (18%)
  starting transfers between devices  16.8 us (12%)
  between operations  13.5 us (10%)
  matrix products  5.7 us (4%)
  other arithmetic  5.35 us (4%)
    all_to_all x1, waiting for transfers between devices, per_device(): lax.all_to_all(green_k, 'img', split_axis=4, concat_axis=0, tiled=True)  33.5 us
    all_to_all x1, blocking collectives, per_device(): lax.all_to_all(summed, 'img', split_axis=0, concat_axis=3, tiled=True)  25.3 us
    unnamed x7, local copies, waits for them, and re-layouts  16.8 us
    all_to_all x1, starting transfers between devices, per_device(): lax.all_to_all(green_k, 'img', split_axis=4, concat_axis=0, tiled=True)  16.8 us
    all_to_all x2, local copies, waits for them, and re-layouts, per_device(): lax.all_to_all(green_k, 'img', split_axis=4, concat_axis=0, tiled=True)  6.52 us
    all_to_all x2, local copies, waits for them, and re-layouts, per_device(): lax.all_to_all(summed, 'img', split_axis=0, concat_axis=3, tiled=True)  5.27 us
    slice x2, local copies, waits for them, and re-layouts, per_device(): imag_part = block[:, :, 1].reshape(count, -1)  5.22 us
    dot_general x1, matrix products, per_device(): jnp.einsum('rtij,rjk->rtik', green_low, integral, preferred_element_type=...  3.94 us
  transfers between devices with their start and end apart: 2, of which 1 were waited for; matrix products, arithmetic and copies ran while one was open for 32% of the time, Pallas kernels for 0%

commit v1 on v0

v1 whole, which is shorter than its diff:
```python
import functools

import jax
import jax.numpy as jnp
from jax import lax
from jax.experimental import pallas as pl
from jax.experimental.pallas import tpu as pltpu
from jax.sharding import PartitionSpec as P

TAU = 8
LANES = 128
HALF = 8
SIDE = 4
VMEM = pl.BlockSpec(memory_space=pltpu.VMEM)
LIMIT = 16 * 1024 * 1024


def params(limit=LIMIT):
    return pltpu.CompilerParams(vmem_limit_bytes=limit)


def cost(flops, moved):
    return pl.CostEstimate(flops=flops, bytes_accessed=moved, transcendentals=0)


def pack_kernel(band_ref, green_ref, fit_ref, packed_ref, factor_ref):
    for t in range(TAU):
        for ih in range(2):
            rows = slice(ih * HALF, (ih + 1) * HALF)
            for jh in range(2):
                cols = slice(jh * LANES, (jh + 1) * LANES)
                both = green_ref[0, t, :, rows, cols].reshape(2 * HALF, LANES)
                packed_ref[(t * 2 + ih) * 2 + jh] = both.astype(jnp.bfloat16)
    factor_ref[...] = fit_ref[...]


def pack(green_k, band, fit):
    points = green_k.shape[0]
    return pl.pallas_call(
        pack_kernel,
        grid_spec=pltpu.PrefetchScalarGridSpec(
            num_scalar_prefetch=1,
            grid=(points,),
            in_specs=[
                pl.BlockSpec((1,) + green_k.shape[1:], lambda p, band: (p, 0, 0, 0, 0)),
                pl.BlockSpec((1,) + fit.shape[1:], lambda p, band: (band[p], 0, 0)),
            ],
            out_specs=[
                pl.BlockSpec((32, 2 * HALF, LANES), lambda p, band: (0, p, 0)),
                pl.BlockSpec((1,) + fit.shape[1:], lambda p, band: (p, 0, 0)),
            ],
        ),
        out_shape=[
            jax.ShapeDtypeStruct((32, points * 2 * HALF, LANES), jnp.bfloat16),
            jax.ShapeDtypeStruct((points,) + fit.shape[1:], fit.dtype),
        ],
        compiler_params=params(),
        cost_estimate=cost(2**18, 2**20),
        name="pack",
    )(band, green_k, fit)


def add(a, b):
    return (a[0] + b[0], a[1] + b[1])


def sub(a, b):
    return (a[0] - b[0], a[1] - b[1])


def turn(a):
    return (-a[1], a[0])


def transform_kernel(x_ref, out_ref, mid_ref):
    for k1 in range(8):
        point = []
        for k2 in range(4):
            rows = x_ref[k1 * 4 + k2].astype(jnp.float32).reshape(4, HALF, LANES)
            a, b = (rows[0], rows[1]), (rows[2], rows[3])
            point.append((add(a, b), sub(a, b)))
        for r3 in range(2):
            y0, y1, y2, y3 = (point[k2][r3] for k2 in range(4))
            s02, d02, s13, d13 = add(y0, y2), sub(y0, y2), add(y1, y3), turn(sub(y1, y3))
            for r2, value in enumerate((add(s02, s13), add(d02, d13), sub(s02, s13), sub(d02, d13))):
                mid_ref[k1, r2, r3, 0] = value[0]
                mid_ref[k1, r2, r3, 1] = value[1]
    root = 0.5**0.5
    scale = 1.0 / 64.0
    for r2 in range(4):
        images = []
        for r3 in range(2):
            re = [mid_ref[k1, r2, r3, 0] for k1 in range(8)]
            im = [mid_ref[k1, r2, r3, 1] for k1 in range(8)]
            p1, p2, p3 = re[1] + re[7], re[2] + re[6], re[3] + re[5]
            q1, q2, q3 = im[1] - im[7], im[2] - im[6], im[3] - im[5]
            even, odd = re[0] + re[4], re[0] - re[4]
            pp, qq = p1 + p3, q1 - q3
            pm, qp = root * (p1 - p3), root * (q1 + q3)
            e_plus, e_minus = even + p2, even - p2
            h0, h1 = odd + pm, odd - pm
            g0, g1 = qp + q2, qp - q2
            images.append(
                (e_plus + pp, h0 - g0, e_minus - qq, h1 - g1, e_plus - pp, h1 + g1, e_minus + qq, h0 + g0)
            )
        for r1 in range(8):
            pair = jnp.concatenate([images[0][r1], images[1][r1]], axis=0) * scale
            out_ref[r1 * 4 + r2] = pair.astype(jnp.bfloat16)


def transform(x):
    return pl.pallas_call(
        transform_kernel,
        in_specs=[VMEM],
        out_specs=VMEM,
        out_shape=jax.ShapeDtypeStruct((32, 2 * HALF, LANES), jnp.bfloat16),
        scratch_shapes=[pltpu.VMEM((8, 4, 2, 2, HALF, LANES), jnp.float32)],
        compiler_params=params(),
        cost_estimate=cost(2**20, 2**20),
        name="transform",
    )(x)


def gram(a, b):
    return lax.dot_general(a, b, (((0,), (0,)), ((), ())), preferred_element_type=jnp.float32)


def partial_kernel(*refs):
    out_ref = refs[-1]
    for s in range(2):
        whole = jnp.concatenate([ref[s] for ref in refs[:-1]], axis=0)
        left, right = whole[:, :LANES], whole[:, LANES:]
        out_ref[s, 0] = gram(left, left)
        out_ref[s, 1] = gram(left, right)
        out_ref[s, 2] = gram(right, right)


def partial_integral(factors):
    return pl.pallas_call(
        partial_kernel,
        in_specs=[VMEM] * len(factors),
        out_specs=VMEM,
        out_shape=jax.ShapeDtypeStruct((2, 3, LANES, LANES), jnp.float32),
        compiler_params=params(),
        cost_estimate=cost(2**27, 2**20),
        name="partial_integral",
    )(*factors)


def sigma_kernel(images_ref, *refs):
    out_ref = refs[-1]
    parts = refs[:-1]
    for s in range(2):
        total = parts[0][s]
        for part in parts[1:]:
            total = total + part[s]
        total = total.astype(jnp.bfloat16)
        green = []
        for jh in range(2):
            tiles = []
            for t in range(TAU):
                for ih in range(2):
                    tile = images_ref[(t * 2 + ih) * 2 + jh].astype(jnp.float32)
                    tiles.append(tile[s * HALF : (s + 1) * HALF])
            green.append(tiles)
        first, second = (jnp.concatenate(tiles, axis=0).astype(jnp.bfloat16) for tiles in green)
        left = (
            jnp.dot(first, total[0], preferred_element_type=jnp.float32)
            + lax.dot_general(second, total[1], (((1,), (1,)), ((), ())), preferred_element_type=jnp.float32),
            jnp.dot(first, total[1], preferred_element_type=jnp.float32)
            + jnp.dot(second, total[2], preferred_element_type=jnp.float32),
        )
        for jh in range(2):
            for t in range(TAU):
                for ih in range(2):
                    at = (t * 2 + ih) * HALF
                    back = green[jh][(TAU - 1 - t) * 2 + ih]
                    out_ref[s, t, ih * HALF : (ih + 1) * HALF, jh * LANES : (jh + 1) * LANES] = (
                        left[jh][at : at + HALF] * back
                    )


def self_energy(images, parts):
    return pl.pallas_call(
        sigma_kernel,
        in_specs=[VMEM] * (1 + len(parts)),
        out_specs=VMEM,
        out_shape=jax.ShapeDtypeStruct((2, TAU, 2 * HALF, 2 * LANES), jnp.float32),
        compiler_params=params(),
        cost_estimate=cost(2**26, 2**20),
        name="self_energy",
    )(images, *parts)


def along_x(value, step):
    pairs = [(o, o // SIDE * SIDE + (o + step) % SIDE) for o in range(SIDE * SIDE)]
    return lax.ppermute(value, "orb", pairs)


def along_y(value, step):
    pairs = [(o, (o + step * SIDE) % (SIDE * SIDE)) for o in range(SIDE * SIDE)]
    return lax.ppermute(value, "orb", pairs)


def per_device(green_k, band_of_image, fit_tensor):
    packed, factor = pack(green_k, band_of_image, fit_tensor)
    factors = [factor] + [along_x(factor, step) for step in (1, 2, 3)]
    block = lax.all_to_all(packed, "img", 0, 0, tiled=True)
    part = partial_integral(factors)
    parts = [part] + [along_y(part, step) for step in (1, 2, 3)]
    images = lax.all_to_all(transform(block), "img", 0, 0, tiled=True)
    return self_energy(images, parts)


def solution(mesh):
    return jax.shard_map(
        per_device,
        mesh=mesh,
        in_specs=(P("img", None, None, "orb", None), P("img"), P(None, "orb", None)),
        out_specs=P("img", None, "orb", None),
        check_vma=False,
    )
```

time: 141 us -> 78 us (0.55)
  local copies, waits for them, and re-layouts: 40.1 us -> 3.29 us
  blocking collectives: 25.3 us -> 0 us
  starting transfers between devices: 16.8 us -> 40.1 us
  between operations: 13.5 us -> 0.1 us
  matrix products: 5.7 us -> 0 us
  other arithmetic: 5.35 us -> 0 us
  Pallas kernels: 0 us -> 3.41 us
  waiting for transfers between devices: 33.5 us -> 30.6 us
    all_to_all x1 -> x0, blocking collectives: 25.3 us -> none  [per_device(): lax.all_to_all(summed, 'img', split_axis=0, concat_axis=3, tiled=True)]
    all_to_all x1 -> x2, waiting for transfers between devices: 33.5 us -> 12.6 us  [the longest x1 12.6 us: per_device(): block = lax.all_to_all(packed, 'img', 0, 0, tiled=True)]
    ppermute x0 -> x6, starting transfers between devices: none -> 18.8 us  [the longest x3 9.5 us: along_y(): return lax.ppermute(value, 'orb', pairs)]
    ppermute x0 -> x6, waiting for transfers between devices: none -> 18 us  [the longest x3 18 us: along_y(): return lax.ppermute(value, 'orb', pairs)]
    unnamed x7 -> x6, local copies, waits for them, and re-layouts: 16.8 us -> 3.29 us
    all_to_all x4 -> x0, local copies, waits for them, and re-layouts: 11.8 us -> none  [the longest x2 6.52 us: per_device(): lax.all_to_all(green_k, 'img', split_axis=4, concat_axis=0, tiled=True)]
    slice x3 -> x0, local copies, waits for them, and re-layouts: 7.91 us -> none  [the longest x2 5.22 us: per_device(): imag_part = block[:, :, 1].reshape(count, -1)]
    dot_general x3 -> x0, matrix products: 5.7 us -> none  [the longest x1 3.94 us: per_device(): jnp.einsum('rtij,rjk->rtik', green_low, integral, preferred_element_type=...]
  transfers between devices with their start and end apart: 2 -> 8, of which waited for: 1 -> 3; matrix products, arithmetic and copies ran while one was open for 32% -> 0% of each run, Pallas kernels for 0% -> 2%
where the time goes in v1:
time: 78 us; the launch traced here: 77.5 us
  starting transfers between devices  40.1 us (51%)
  waiting for transfers between devices  30.6 us (39%)
  Pallas kernels  3.41 us (4%)
  local copies, waits for them, and re-layouts  3.29 us (4%)
    ppermute x3, waiting for transfers between devices, along_y(): return lax.ppermute(value, 'orb', pairs)  18 us
    all_to_all x1, starting transfers between devices, per_device(): block = lax.all_to_all(packed, 'img', 0, 0, tiled=True)  16.7 us
    all_to_all x1, waiting for transfers between devices, per_device(): block = lax.all_to_all(packed, 'img', 0, 0, tiled=True)  12.6 us
    ppermute x3, starting transfers between devices, along_y(): return lax.ppermute(value, 'orb', pairs)  9.5 us
    ppermute x3, starting transfers between devices, along_x(): return lax.ppermute(value, 'orb', pairs)  9.33 us
    all_to_all x1, starting transfers between devices, per_device(): images = lax.all_to_all(transform(block), 'img', 0, 0, tiled=True)  4.51 us
    unnamed x6, local copies, waits for them, and re-layouts  3.29 us
  transfers between devices with their start and end apart: 8, of which 3 were waited for; matrix products, arithmetic and copies ran while one was open for 0% of the time, Pallas kernels for 2%

profile of v1, /device:TPU:1, one launch (start us, length us, event | category | flops | bytes accessed | tf_op | source)
XLA Modules:
  0.0 77.5 jit_solution(3979773631026190827)
XLA Ops:
  0.0 0.0 copy-start
  0.0 1.6 %copy-done = bf16[32,128,256]{2,1,0:T(8,128)(2,1)S(1)} copy-done((bf16[32,128,256]{2,1,0:T(8,128)(2,1)S(1)}, bf16[32,128,256]{2,1,0:T(8,128)(2,1)}, u32[]{:S(2)}) %copy-start) | copy-done | bytes 2097176
  1.6 1.0 %copy-done.1 = f32[2,8,2,16,256]{4,3,2,1,0:T(8,128)S(1)} copy-done((f32[2,8,2,16,256]{4,3,2,1,0:T(8,128)S(1)}, f32[2,8,2,16,256]{4,3,2,1,0:T(8,128)}, u32[]{:S(2)}) %copy-start.1) | copy-done | bytes 524312
  2.6 0.7 copy-done.2
  3.3 1.3 %pack.1 = (bf16[32,32,128]{2,1,0:T(8,128)(2,1)}, bf16[2,128,256]{2,1,0:T(8,128)(2,1)S(1)}) custom-call(s32[2]{0:T(128)S(1)} %copy-done.2, f32[2,8,2,16,256]{4,3,2,1,0:T(8,128)S(1)} %copy-done.1, bf16[32,128,256]{2,1,0:T(8,128)(2,1)S(1)} %copy-done), custom_call_target="tpu_custom_call" | custom-call | flops 262144 | bytes 1048576 | tf_op jit(solution)/shard_map/pack/pallas_call | solution.py:39
  4.6 16.7 %all-to-all-start = ((bf16[32,32,128]{2,1,0:T(8,128)(2,1)}), bf16[32,32,128]{2,1,0:T(8,128)(2,1)S(1)}, u32[]{:S(2)}, u32[]{:S(2)}) async-start(bf16[32,32,128]{2,1,0:T(8,128)(2,1)} %get-tuple-element.7), calls=%async_computation | async-start | bytes 524288 | tf_op jit(solution)/shard_map/all_to_all | solution.py:208
  21.3 4.4 %collective-permute-start.2 = (bf16[2,128,256]{2,1,0:T(8,128)(2,1)S(1)}, bf16[2,128,256]{2,1,0:T(8,128)(2,1)S(1)}, u32[]{:S(2)}, u32[]{:S(2)}) collective-permute-start(bf16[2,128,256]{2,1,0:T(8,128)(2,1)S(1)} %get-tuple-element.8.refs_0_), channel_id=1, source_target_pairs={{0,3},{1,0},{2,1},{3,2},{4,7},{5,4},{6,5},{7,6},{8,11},{9,8},{10,9... | collective-permute-start | bytes 393224 | tf_op jit(solution)/shard_map/ppermute | solution.py:197
  25.7 2.4 %collective-permute-start.1 = (bf16[2,128,256]{2,1,0:T(8,128)(2,1)S(1)}, bf16[2,128,256]{2,1,0:T(8,128)(2,1)S(1)}, u32[]{:S(2)}, u32[]{:S(2)}) collective-permute-start(bf16[2,128,256]{2,1,0:T(8,128)(2,1)S(1)} %get-tuple-element.8.refs_0_), channel_id=1, source_target_pairs={{0,2},{1,3},{2,0},{3,1},{4,6},{5,7},{6,4},{7,5},{8,10},{9,11},{10,... | collective-permute-start | bytes 393224 | tf_op jit(solution)/shard_map/ppermute | solution.py:197
  28.2 2.5 %collective-permute-start = (bf16[2,128,256]{2,1,0:T(8,128)(2,1)S(1)}, bf16[2,128,256]{2,1,0:T(8,128)(2,1)S(1)}, u32[]{:S(2)}, u32[]{:S(2)}) collective-permute-start(bf16[2,128,256]{2,1,0:T(8,128)(2,1)S(1)} %get-tuple-element.8.refs_0_), channel_id=1, source_target_pairs={{0,1},{1,2},{2,3},{3,0},{4,5},{5,6},{6,7},{7,4},{8,9},{9,10},{10,1... | collective-permute-start | bytes 393224 | tf_op jit(solution)/shard_map/ppermute | solution.py:197
  30.7 12.6 %all-to-all-done.x_ref = bf16[32,32,128]{2,1,0:T(8,128)(2,1)S(1)} async-done(((bf16[32,32,128]{2,1,0:T(8,128)(2,1)}), bf16[32,32,128]{2,1,0:T(8,128)(2,1)S(1)}, u32[]{:S(2)}, u32[]{:S(2)}) %all-to-all-start) | async-done | bytes 262176 | tf_op jit(solution)/shard_map/all_to_all | solution.py:208
  43.3 0.8 %transform.1 = bf16[32,16,128]{2,1,0:T(8,128)(2,1)} custom-call(bf16[32,32,128]{2,1,0:T(8,128)(2,1)S(1)} %all-to-all-done.x_ref), custom_call_target="tpu_custom_call" | custom-call | flops 1048576 | bytes 1048576 | tf_op jit(solution)/shard_map/transform/pallas_call | solution.py:112
  44.1 4.5 %all-to-all-start.1 = ((bf16[32,16,128]{2,1,0:T(8,128)(2,1)}), bf16[32,16,128]{2,1,0:T(8,128)(2,1)S(1)}, u32[]{:S(2)}, u32[]{:S(2)}) async-start(bf16[32,16,128]{2,1,0:T(8,128)(2,1)} %transform.1), calls=%async_computation.1 | async-start | bytes 262144 | tf_op jit(solution)/shard_map/all_to_all | solution.py:211
  48.6 0.0 collective-permute-done.2.refs_3_
  48.6 0.0 collective-permute-done.1.refs_2_
  48.6 0.0 collective-permute-done.refs_1_
  48.7 0.4 partial_integral.1.refs_0_
  49.1 4.6 %collective-permute-start.5 = (f32[2,3,128,128]{3,2,1,0:T(8,128)S(1)}, f32[2,3,128,128]{3,2,1,0:T(8,128)S(1)}, u32[]{:S(2)}, u32[]{:S(2)}) collective-permute-start(f32[2,3,128,128]{3,2,1,0:T(8,128)S(1)} %partial_integral.1.refs_0_), channel_id=1, source_target_pairs={{0,12},{1,13},{2,14},{3,15},{4,0},{5,1},{6,2},{7,3},{8,4},{9,5},{1... | collective-permute-start | bytes 1179656 | tf_op jit(solution)/shard_map/ppermute | solution.py:202
  53.7 2.3 %collective-permute-start.4 = (f32[2,3,128,128]{3,2,1,0:T(8,128)S(1)}, f32[2,3,128,128]{3,2,1,0:T(8,128)S(1)}, u32[]{:S(2)}, u32[]{:S(2)}) collective-permute-start(f32[2,3,128,128]{3,2,1,0:T(8,128)S(1)} %partial_integral.1.refs_0_), channel_id=1, source_target_pairs={{0,8},{1,9},{2,10},{3,11},{4,12},{5,13},{6,14},{7,15},{8,0},{9,1},... | collective-permute-start | bytes 1179656 | tf_op jit(solution)/shard_map/ppermute | solution.py:202
  56.0 2.6 %collective-permute-start.3 = (f32[2,3,128,128]{3,2,1,0:T(8,128)S(1)}, f32[2,3,128,128]{3,2,1,0:T(8,128)S(1)}, u32[]{:S(2)}, u32[]{:S(2)}) collective-permute-start(f32[2,3,128,128]{3,2,1,0:T(8,128)S(1)} %partial_integral.1.refs_0_), channel_id=1, source_target_pairs={{0,4},{1,5},{2,6},{3,7},{4,8},{5,9},{6,10},{7,11},{8,12},{9,13},{1... | collective-permute-start | bytes 1179656 | tf_op jit(solution)/shard_map/ppermute | solution.py:202
  58.6 11.5 %collective-permute-done.5.refs_3_ = f32[2,3,128,128]{3,2,1,0:T(8,128)S(1)} collective-permute-done((f32[2,3,128,128]{3,2,1,0:T(8,128)S(1)}, f32[2,3,128,128]{3,2,1,0:T(8,128)S(1)}, u32[]{:S(2)}, u32[]{:S(2)}) %collective-permute-start.5) | collective-permute-done | bytes 393248 | tf_op jit(solution)/shard_map/ppermute | solution.py:202
  70.1 0.0 collective-permute-done.4.refs_2_
  70.1 6.5 %collective-permute-done.3.refs_1_ = f32[2,3,128,128]{3,2,1,0:T(8,128)S(1)} collective-permute-done((f32[2,3,128,128]{3,2,1,0:T(8,128)S(1)}, f32[2,3,128,128]{3,2,1,0:T(8,128)S(1)}, u32[]{:S(2)}, u32[]{:S(2)}) %collective-permute-start.3) | collective-permute-done | bytes 393248 | tf_op jit(solution)/shard_map/ppermute | solution.py:202
  76.6 0.0 all-to-all-done.1.images_ref
  76.6 0.9 %self_energy.1 = f32[2,8,16,256]{3,2,1,0:T(8,128)} custom-call(bf16[32,16,128]{2,1,0:T(8,128)(2,1)S(1)} %all-to-all-done.1.images_ref, f32[2,3,128,128]{3,2,1,0:T(8,128)S(1)} %partial_integral.1.refs_0_, f32[2,3,128,128]{3,2,1,0:T(8,128)S(1)} %collective-permute-done.3.refs_1_, f32[2,3,128,128]{3,2,1,0:T(8,128)S(1)} %collective-permute-done.4.refs_2_, ...), custom_call_target="tpu_custom_call" | custom-call | flops 67108864 | bytes 1048576 | tf_op jit(solution)/shard_map/self_energy/pallas_call | solution.py:184
  (2 shorter events, 0.0 us)
Async XLA Ops:
  0.0 1.6 %copy-start = (bf16[32,128,256]{2,1,0:T(8,128)(2,1)S(1)}, bf16[32,128,256]{2,1,0:T(8,128)(2,1)}, u32[]{:S(2)}) copy-start(bf16[32,128,256]{2,1,0:T(8,128)(2,1)} %fit_ref.1) | copy-start | bytes 6291460
  1.6 1.0 %copy-start.1 = (f32[2,8,2,16,256]{4,3,2,1,0:T(8,128)S(1)}, f32[2,8,2,16,256]{4,3,2,1,0:T(8,128)}, u32[]{:S(2)}) copy-start(f32[2,8,2,16,256]{4,3,2,1,0:T(8,128)} %green_ref.1) | copy-start | bytes 1572868
  2.6 0.7 copy-start.2
  4.6 38.8 %all-to-all-start = ((bf16[32,32,128]{2,1,0:T(8,128)(2,1)}), bf16[32,32,128]{2,1,0:T(8,128)(2,1)S(1)}, u32[]{:S(2)}, u32[]{:S(2)}) async-start(bf16[32,32,128]{2,1,0:T(8,128)(2,1)} %get-tuple-element.7), calls=%async_computation | async-start | bytes 524288 | tf_op jit(solution)/shard_map/all_to_all | solution.py:208
  21.3 27.3 %collective-permute-start.2 = (bf16[2,128,256]{2,1,0:T(8,128)(2,1)S(1)}, bf16[2,128,256]{2,1,0:T(8,128)(2,1)S(1)}, u32[]{:S(2)}, u32[]{:S(2)}) collective-permute-start(bf16[2,128,256]{2,1,0:T(8,128)(2,1)S(1)} %get-tuple-element.8.refs_0_), channel_id=1, source_target_pairs={{0,3},{1,0},{2,1},{3,2},{4,7},{5,4},{6,5},{7,6},{8,11},{9,8},{10,9... | collective-permute-start | bytes 393224 | tf_op jit(solution)/shard_map/ppermute | solution.py:197
  25.7 22.9 %collective-permute-start.1 = (bf16[2,128,256]{2,1,0:T(8,128)(2,1)S(1)}, bf16[2,128,256]{2,1,0:T(8,128)(2,1)S(1)}, u32[]{:S(2)}, u32[]{:S(2)}) collective-permute-start(bf16[2,128,256]{2,1,0:T(8,128)(2,1)S(1)} %get-tuple-element.8.refs_0_), channel_id=1, source_target_pairs={{0,2},{1,3},{2,0},{3,1},{4,6},{5,7},{6,4},{7,5},{8,10},{9,11},{10,... | collective-permute-start | bytes 393224 | tf_op jit(solution)/shard_map/ppermute | solution.py:197
  28.2 20.5 %collective-permute-start = (bf16[2,128,256]{2,1,0:T(8,128)(2,1)S(1)}, bf16[2,128,256]{2,1,0:T(8,128)(2,1)S(1)}, u32[]{:S(2)}, u32[]{:S(2)}) collective-permute-start(bf16[2,128,256]{2,1,0:T(8,128)(2,1)S(1)} %get-tuple-element.8.refs_0_), channel_id=1, source_target_pairs={{0,1},{1,2},{2,3},{3,0},{4,5},{5,6},{6,7},{7,4},{8,9},{9,10},{10,1... | collective-permute-start | bytes 393224 | tf_op jit(solution)/shard_map/ppermute | solution.py:197
  44.1 32.5 %all-to-all-start.1 = ((bf16[32,16,128]{2,1,0:T(8,128)(2,1)}), bf16[32,16,128]{2,1,0:T(8,128)(2,1)S(1)}, u32[]{:S(2)}, u32[]{:S(2)}) async-start(bf16[32,16,128]{2,1,0:T(8,128)(2,1)} %transform.1), calls=%async_computation.1 | async-start | bytes 262144 | tf_op jit(solution)/shard_map/all_to_all | solution.py:211
  49.1 21.1 %collective-permute-start.5 = (f32[2,3,128,128]{3,2,1,0:T(8,128)S(1)}, f32[2,3,128,128]{3,2,1,0:T(8,128)S(1)}, u32[]{:S(2)}, u32[]{:S(2)}) collective-permute-start(f32[2,3,128,128]{3,2,1,0:T(8,128)S(1)} %partial_integral.1.refs_0_), channel_id=1, source_target_pairs={{0,12},{1,13},{2,14},{3,15},{4,0},{5,1},{6,2},{7,3},{8,4},{9,5},{1... | collective-permute-start | bytes 1179656 | tf_op jit(solution)/shard_map/ppermute | solution.py:202
  53.7 16.4 %collective-permute-start.4 = (f32[2,3,128,128]{3,2,1,0:T(8,128)S(1)}, f32[2,3,128,128]{3,2,1,0:T(8,128)S(1)}, u32[]{:S(2)}, u32[]{:S(2)}) collective-permute-start(f32[2,3,128,128]{3,2,1,0:T(8,128)S(1)} %partial_integral.1.refs_0_), channel_id=1, source_target_pairs={{0,8},{1,9},{2,10},{3,11},{4,12},{5,13},{6,14},{7,15},{8,0},{9,1},... | collective-permute-start | bytes 1179656 | tf_op jit(solution)/shard_map/ppermute | solution.py:202
  56.0 20.6 %collective-permute-start.3 = (f32[2,3,128,128]{3,2,1,0:T(8,128)S(1)}, f32[2,3,128,128]{3,2,1,0:T(8,128)S(1)}, u32[]{:S(2)}, u32[]{:S(2)}) collective-permute-start(f32[2,3,128,128]{3,2,1,0:T(8,128)S(1)} %partial_integral.1.refs_0_), channel_id=1, source_target_pairs={{0,4},{1,5},{2,6},{3,7},{4,8},{5,9},{6,10},{7,11},{8,12},{9,13},{1... | collective-permute-start | bytes 1179656 | tf_op jit(solution)/shard_map/ppermute | solution.py:202

commit v2 on v1

--- a/solution.py
+++ b/solution.py
@@ -1,5 +1,3 @@
-import functools
-
 import jax
 import jax.numpy as jnp
 from jax import lax
@@ -12,6 +10,10 @@
 HALF = 8
 SIDE = 4
 VMEM = pl.BlockSpec(memory_space=pltpu.VMEM)
+HBM = pl.BlockSpec(memory_space=pltpu.HBM)
+CHIPS = (11,10,9,8,7,6,5,4,3,2,1,0,15,14,13,12)
+ORDER = [2 * z + core for core in range(2) for z in CHIPS]
+PLACE = [ORDER.index(img) for img in range(32)]
 LIMIT = 16 * 1024 * 1024
 
 
@@ -23,38 +25,49 @@
     return pl.CostEstimate(flops=flops, bytes_accessed=moved, transcendentals=0)
 
 
-def pack_kernel(band_ref, green_ref, fit_ref, packed_ref, factor_ref):
-    for t in range(TAU):
-        for ih in range(2):
-            rows = slice(ih * HALF, (ih + 1) * HALF)
-            for jh in range(2):
-                cols = slice(jh * LANES, (jh + 1) * LANES)
-                both = green_ref[0, t, :, rows, cols].reshape(2 * HALF, LANES)
-                packed_ref[(t * 2 + ih) * 2 + jh] = both.astype(jnp.bfloat16)
-    factor_ref[...] = fit_ref[...]
+def pack_kernel(band_hbm, green_hbm, fit_hbm, packed_ref, factor_ref, band, green, sems):
+    points = green.shape[0]
+    bands = pltpu.make_async_copy(band_hbm, band, sems.at[2 * points])
+    bands.start()
+    loads = [pltpu.make_async_copy(green_hbm.at[p], green.at[p], sems.at[p]) for p in range(points)]
+    for load in loads:
+        load.start()
+    bands.wait()
+    fits = []
+    for p in range(points):
+        fits.append(pltpu.make_async_copy(fit_hbm.at[band[p]], factor_ref.at[p], sems.at[points + p]))
+        fits[p].start()
+    for p in range(points):
+        loads[p].wait()
+        for t in range(TAU):
+            for ih in range(2):
+                rows = slice(ih * HALF, (ih + 1) * HALF)
+                for jh in range(2):
+                    cols = slice(jh * LANES, (jh + 1) * LANES)
+                    both = green[p, t, :, rows, cols].reshape(2 * HALF, LANES)
+                    packed_ref[(t * 2 + ih) * 2 + jh, 2 * HALF * p : 2 * HALF * (p + 1), :] = both.astype(
+                        jnp.bfloat16
+                    )
+    for fit in fits:
+        fit.wait()
 
 
 def pack(green_k, band, fit):
     points = green_k.shape[0]
     return pl.pallas_call(
         pack_kernel,
-        grid_spec=pltpu.PrefetchScalarGridSpec(
-            num_scalar_prefetch=1,
-            grid=(points,),
-            in_specs=[
-                pl.BlockSpec((1,) + green_k.shape[1:], lambda p, band: (p, 0, 0, 0, 0)),
-                pl.BlockSpec((1,) + fit.shape[1:], lambda p, band: (band[p], 0, 0)),
-            ],
-            out_specs=[
-                pl.BlockSpec((32, 2 * HALF, LANES), lambda p, band: (0, p, 0)),
-                pl.BlockSpec((1,) + fit.shape[1:], lambda p, band: (p, 0, 0)),
-            ],
-        ),
+        in_specs=[HBM] * 3,
+        out_specs=[VMEM] * 2,
         out_shape=[
             jax.ShapeDtypeStruct((32, points * 2 * HALF, LANES), jnp.bfloat16),
             jax.ShapeDtypeStruct((points,) + fit.shape[1:], fit.dtype),
         ],
-        compiler_params=params(),
+        scratch_shapes=[
+            pltpu.SMEM(band.shape, jnp.int32),
+            pltpu.VMEM(green_k.shape, jnp.float32),
+            pltpu.SemaphoreType.DMA((2 * points + 1,)),
+        ],
+        compiler_params=params(60 * 1024 * 1024),
         cost_estimate=cost(2**18, 2**20),
         name="pack",
     )(band, green_k, fit)
@@ -76,7 +89,7 @@
     for k1 in range(8):
         point = []
         for k2 in range(4):
-            rows = x_ref[k1 * 4 + k2].astype(jnp.float32).reshape(4, HALF, LANES)
+            rows = x_ref[PLACE[k1 * 4 + k2]].astype(jnp.float32).reshape(4, HALF, LANES)
             a, b = (rows[0], rows[1]), (rows[2], rows[3])
             point.append((add(a, b), sub(a, b)))
         for r3 in range(2):
@@ -105,7 +118,7 @@
             )
         for r1 in range(8):
             pair = jnp.concatenate([images[0][r1], images[1][r1]], axis=0) * scale
-            out_ref[r1 * 4 + r2] = pair.astype(jnp.bfloat16)
+            out_ref[PLACE[r1 * 4 + r2]] = pair.astype(jnp.bfloat16)
 
 
 def transform(x):
@@ -192,24 +205,36 @@
     )(images, *parts)
 
 
-def along_x(value, step):
-    pairs = [(o, o // SIDE * SIDE + (o + step) % SIDE) for o in range(SIDE * SIDE)]
-    return lax.ppermute(value, "orb", pairs)
-
-
-def along_y(value, step):
-    pairs = [(o, (o + step * SIDE) % (SIDE * SIDE)) for o in range(SIDE * SIDE)]
-    return lax.ppermute(value, "orb", pairs)
+def lines():
+    groups = []
+    for img in range(32):
+        for at in range(SIDE):
+            first, step = (at * SIDE, 1) if img % 2 == 0 else (at, SIDE)
+            groups.append([img * SIDE * SIDE + first + step * i for i in range(SIDE)])
+    return groups
+
+
+def exchanged(value, move, turned):
+    pairs = []
+    for img in range(32):
+        for orb in range(SIDE * SIDE):
+            y, x = divmod(orb, SIDE)
+            if (img + turned) % 2 == 0:
+                x = move(x) % SIDE
+            else:
+                y = move(y) % SIDE
+            pairs.append((img * SIDE * SIDE + orb, img * SIDE * SIDE + y * SIDE + x))
+    return lax.ppermute(value, ("img", "orb"), pairs)
 
 
 def per_device(green_k, band_of_image, fit_tensor):
     packed, factor = pack(green_k, band_of_image, fit_tensor)
-    factors = [factor] + [along_x(factor, step) for step in (1, 2, 3)]
-    block = lax.all_to_all(packed, "img", 0, 0, tiled=True)
-    part = partial_integral(factors)
-    parts = [part] + [along_y(part, step) for step in (1, 2, 3)]
-    images = lax.all_to_all(transform(block), "img", 0, 0, tiled=True)
-    return self_energy(images, parts)
+    block = lax.all_to_all(packed, "img", 0, 0, tiled=True, axis_index_groups=[ORDER])
+    part = partial_integral([lax.all_gather(factor, ("img", "orb"), axis=1, tiled=True, axis_index_groups=lines())])
+    pair = part + exchanged(part, lambda at: at ^ 1, 1)
+    other = exchanged(pair, lambda at: at + 1 if at % 2 else at - 1, 1)
+    images = lax.all_to_all(transform(block), "img", 0, 0, tiled=True, axis_index_groups=[ORDER])
+    return self_energy(images, [pair, other])
 
 
 def solution(mesh):

time: 78 us -> 61.4 us (0.79)
  waiting for transfers between devices: 30.6 us -> 5.99 us
  blocking collectives: 0 us -> 11.5 us
  local copies, waits for them, and re-layouts: 3.29 us -> 0 us
  starting transfers between devices: 40.1 us -> 39 us
  Pallas kernels: 3.41 us -> 4.47 us
    all_to_all x2, waiting for transfers between devices: 12.6 us -> 0.01 us  [the longest x1 0.01 us: per_device(): lax.all_to_all(packed, 'img', 0, 0, tiled=True, axis_index_groups=[ORDER])]
    ppermute x6 -> x2, waiting for transfers between devices: 18 us -> 5.98 us  [exchanged(): return lax.ppermute(value, ('img', 'orb'), pairs)]
    ppermute x6 -> x2, starting transfers between devices: 18.8 us -> 7.16 us  [exchanged(): return lax.ppermute(value, ('img', 'orb'), pairs)]
    all_gather x0 -> x1, blocking collectives: none -> 11.5 us  [per_device(): lax.all_gather(factor, ('img', 'orb'), axis=1, tiled=True, axis_index_gro...]
    all_to_all x2, starting transfers between devices: 21.3 us -> 31.9 us  [the longest x1 17.5 us: per_device(): lax.all_to_all(packed, 'img', 0, 0, tiled=True, axis_index_groups=[ORDER])]
    unnamed x6 -> x0, local copies, waits for them, and re-layouts: 3.29 us -> none
    pallas_call x1, Pallas kernels: 1.29 us -> 2.34 us  [pack(): pl.pallas_call(pack_kernel, in_specs=[HBM] * 3, out_specs=[VMEM] * 2, out...]
  transfers between devices with their start and end apart: 8 -> 4, of which waited for: 3 -> 1; matrix products, arithmetic and copies ran while one was open for 0% -> 0% of each run, Pallas kernels for 2% -> 2%
where the time goes in v2:
time: 61.4 us; the launch traced here: 61.1 us
  starting transfers between devices  39 us (64%)
  blocking collectives  11.5 us (19%)
  waiting for transfers between devices  5.99 us (10%)
  Pallas kernels  4.47 us (7%)
    all_to_all x1, starting transfers between devices, per_device(): lax.all_to_all(packed, 'img', 0, 0, tiled=True, axis_index_groups=[ORDER])  17.5 us
    all_to_all x1, starting transfers between devices, per_device(): lax.all_to_all(transform(block), 'img', 0, 0, tiled=True, axis_index_grou...  14.4 us
    all_gather x1, blocking collectives, per_device(): lax.all_gather(factor, ('img', 'orb'), axis=1, tiled=True, axis_index_gro...  11.5 us
    ppermute x2, starting transfers between devices, exchanged(): return lax.ppermute(value, ('img', 'orb'), pairs)  7.16 us
    ppermute x2, waiting for transfers between devices, exchanged(): return lax.ppermute(value, ('img', 'orb'), pairs)  5.98 us
    pallas_call x1, Pallas kernels, pack(): pl.pallas_call(pack_kernel, in_specs=[HBM] * 3, out_specs=[VMEM] * 2, out...  2.34 us
  transfers between devices with their start and end apart: 4, of which 1 were waited for; matrix products, arithmetic and copies ran while one was open for 0% of the time, Pallas kernels for 2%

profile of v2, /device:TPU:1, one launch (start us, length us, event | category | flops | bytes accessed | tf_op | source)
XLA Modules:
  0.0 61.1 jit_solution(5921056676727880485)
XLA Ops:
  0.0 2.3 %pack.1 = (bf16[32,32,128]{2,1,0:T(8,128)(2,1)}, bf16[2,128,256]{2,1,0:T(8,128)(2,1)}) custom-call(s32[2]{0:T(128)} %band_hbm.1, f32[2,8,2,16,256]{4,3,2,1,0:T(8,128)} %green_hbm.1, bf16[32,128,256]{2,1,0:T(8,128)(2,1)} %fit_hbm.1), custom_call_target="tpu_custom_call" | custom-call | flops 262144 | bytes 1048576 | tf_op jit(solution)/shard_map/pack/pallas_call | solution.py:57
  2.3 17.5 %all-to-all-start = ((bf16[32,32,128]{2,1,0:T(8,128)(2,1)}), bf16[32,32,128]{2,1,0:T(8,128)(2,1)S(1)}, u32[]{:S(2)}, u32[]{:S(2)}) async-start(bf16[32,32,128]{2,1,0:T(8,128)(2,1)} %get-tuple-element.7), calls=%async_computation | async-start | bytes 524288 | tf_op jit(solution)/shard_map/all_to_all | solution.py:232
  19.8 11.5 %all_gather.3.refs_0_ = bf16[2,512,256]{2,1,0:T(8,128)(2,1)S(1)} all-gather(bf16[2,128,256]{2,1,0:T(8,128)(2,1)} %get-tuple-element.8), channel_id=1, replica_groups={{0,1,2,3},{4,5,6,7},{8,9,10,11},{12,13,14,15},{16,20,24,28},{17,21,25,2..., dimensions={1}, use_global_device_ids=true | all-gather | bytes 655360 | tf_op jit(solution)/shard_map/all_gather | solution.py:233
  31.3 0.4 partial_integral.1
  31.8 3.1 %collective-permute-start = (f32[2,3,128,128]{3,2,1,0:T(8,128)S(1)}, f32[2,3,128,128]{3,2,1,0:T(8,128)S(1)}, u32[]{:S(2)}, u32[]{:S(2)}) collective-permute-start(f32[2,3,128,128]{3,2,1,0:T(8,128)S(1)} %partial_integral.1), channel_id=1, source_target_pairs={{0,4},{1,5},{2,6},{3,7},{4,0},{5,1},{6,2},{7,3},{8,12},{9,13},{10,... | collective-permute-start | bytes 1179656 | tf_op jit(solution)/shard_map/ppermute | solution.py:227
  34.9 0.0 all-to-all-done.x_ref
  34.9 0.8 %transform.1 = bf16[32,16,128]{2,1,0:T(8,128)(2,1)} custom-call(bf16[32,32,128]{2,1,0:T(8,128)(2,1)S(1)} %all-to-all-done.x_ref), custom_call_target="tpu_custom_call" | custom-call | flops 1048576 | bytes 1048576 | tf_op jit(solution)/shard_map/transform/pallas_call | solution.py:125
  35.7 14.4 %all-to-all-start.1 = ((bf16[32,16,128]{2,1,0:T(8,128)(2,1)}), bf16[32,16,128]{2,1,0:T(8,128)(2,1)S(1)}, u32[]{:S(2)}, u32[]{:S(2)}) async-start(bf16[32,16,128]{2,1,0:T(8,128)(2,1)} %transform.1), calls=%async_computation.1 | async-start | bytes 262144 | tf_op jit(solution)/shard_map/all_to_all | solution.py:236
  50.1 0.0 collective-permute-done
  50.1 4.0 %collective-permute-start.1 = (f32[2,3,128,128]{3,2,1,0:T(8,128)S(1)}, f32[2,3,128,128]{3,2,1,0:T(8,128)S(1)}, u32[]{:S(2)}, u32[]{:S(2)}) collective-permute-start(f32[2,3,128,128]{3,2,1,0:T(8,128)S(1)} %add.3.refs_0_), channel_id=1, source_target_pairs={{0,12},{1,13},{2,14},{3,15},{4,8},{5,9},{6,10},{7,11},{8,4},{9,5},... | collective-permute-start | bytes 1179656 | tf_op jit(solution)/shard_map/ppermute | solution.py:227
  54.2 6.0 %collective-permute-done.1.refs_1_ = f32[2,3,128,128]{3,2,1,0:T(8,128)S(1)} collective-permute-done((f32[2,3,128,128]{3,2,1,0:T(8,128)S(1)}, f32[2,3,128,128]{3,2,1,0:T(8,128)S(1)}, u32[]{:S(2)}, u32[]{:S(2)}) %collective-permute-start.1) | collective-permute-done | bytes 393248 | tf_op jit(solution)/shard_map/ppermute | solution.py:227
  60.1 0.0 all-to-all-done.1.images_ref
  60.2 0.9 %self_energy.1 = f32[2,8,16,256]{3,2,1,0:T(8,128)} custom-call(bf16[32,16,128]{2,1,0:T(8,128)(2,1)S(1)} %all-to-all-done.1.images_ref, f32[2,3,128,128]{3,2,1,0:T(8,128)S(1)} %add.3.refs_0_, f32[2,3,128,128]{3,2,1,0:T(8,128)S(1)} %collective-permute-done.1.refs_1_), custom_call_target="tpu_custom_call" | custom-call | flops 67108864 | bytes 1048576 | tf_op jit(solution)/shard_map/self_energy/pallas_call | solution.py:197
  (1 shorter events, 0.0 us)
Async XLA Ops:
  2.3 32.5 %all-to-all-start = ((bf16[32,32,128]{2,1,0:T(8,128)(2,1)}), bf16[32,32,128]{2,1,0:T(8,128)(2,1)S(1)}, u32[]{:S(2)}, u32[]{:S(2)}) async-start(bf16[32,32,128]{2,1,0:T(8,128)(2,1)} %get-tuple-element.7), calls=%async_computation | async-start | bytes 524288 | tf_op jit(solution)/shard_map/all_to_all | solution.py:232
  31.8 18.3 %collective-permute-start = (f32[2,3,128,128]{3,2,1,0:T(8,128)S(1)}, f32[2,3,128,128]{3,2,1,0:T(8,128)S(1)}, u32[]{:S(2)}, u32[]{:S(2)}) collective-permute-start(f32[2,3,128,128]{3,2,1,0:T(8,128)S(1)} %partial_integral.1), channel_id=1, source_target_pairs={{0,4},{1,5},{2,6},{3,7},{4,0},{5,1},{6,2},{7,3},{8,12},{9,13},{10,... | collective-permute-start | bytes 1179656 | tf_op jit(solution)/shard_map/ppermute | solution.py:227
  35.7 24.5 %all-to-all-start.1 = ((bf16[32,16,128]{2,1,0:T(8,128)(2,1)}), bf16[32,16,128]{2,1,0:T(8,128)(2,1)S(1)}, u32[]{:S(2)}, u32[]{:S(2)}) async-start(bf16[32,16,128]{2,1,0:T(8,128)(2,1)} %transform.1), calls=%async_computation.1 | async-start | bytes 262144 | tf_op jit(solution)/shard_map/all_to_all | solution.py:236
  50.1 10.0 %collective-permute-start.1 = (f32[2,3,128,128]{3,2,1,0:T(8,128)S(1)}, f32[2,3,128,128]{3,2,1,0:T(8,128)S(1)}, u32[]{:S(2)}, u32[]{:S(2)}) collective-permute-start(f32[2,3,128,128]{3,2,1,0:T(8,128)S(1)} %add.3.refs_0_), channel_id=1, source_target_pairs={{0,12},{1,13},{2,14},{3,15},{4,8},{5,9},{6,10},{7,11},{8,4},{9,5},... | collective-permute-start | bytes 1179656 | tf_op jit(solution)/shard_map/ppermute | solution.py:227

commit v3 on v2

--- a/solution.py
+++ b/solution.py
@@ -11,9 +11,11 @@
 SIDE = 4
 VMEM = pl.BlockSpec(memory_space=pltpu.VMEM)
 HBM = pl.BlockSpec(memory_space=pltpu.HBM)
-CHIPS = (11,10,9,8,7,6,5,4,3,2,1,0,15,14,13,12)
-ORDER = [2 * z + core for core in range(2) for z in CHIPS]
+ORDER = [24, 22, 20, 18, 16, 14, 12, 10, 8, 6, 4, 2, 0, 30, 28, 26, 25, 23, 21, 19, 17, 15, 13, 11, 9, 7, 5, 3, 1, 31, 29, 27]
+BACK_ORDER = [20, 18, 16, 14, 12, 10, 8, 6, 4, 2, 0, 30, 28, 26, 24, 22, 21, 19, 17, 15, 13, 11, 9, 7, 5, 3, 1, 31, 29, 27, 25, 23]
 PLACE = [ORDER.index(img) for img in range(32)]
+BACK_PLACE = [BACK_ORDER.index(img) for img in range(32)]
+CAME = [BACK_PLACE[img] for img in ORDER]
 LIMIT = 16 * 1024 * 1024
 
 
@@ -118,7 +120,7 @@
             )
         for r1 in range(8):
             pair = jnp.concatenate([images[0][r1], images[1][r1]], axis=0) * scale
-            out_ref[PLACE[r1 * 4 + r2]] = pair.astype(jnp.bfloat16)
+            out_ref[BACK_PLACE[r1 * 4 + r2]] = pair.astype(jnp.bfloat16)
 
 
 def transform(x):
@@ -138,50 +140,56 @@
     return lax.dot_general(a, b, (((0,), (0,)), ((), ())), preferred_element_type=jnp.float32)
 
 
-def partial_kernel(*refs):
-    out_ref = refs[-1]
+def partial_kernel(whole_ref, out_ref):
+    row = lax.broadcasted_iota(jnp.int32, (LANES, LANES), 0)
+    col = lax.broadcasted_iota(jnp.int32, (LANES, LANES), 1)
     for s in range(2):
-        whole = jnp.concatenate([ref[s] for ref in refs[:-1]], axis=0)
-        left, right = whole[:, :LANES], whole[:, LANES:]
-        out_ref[s, 0] = gram(left, left)
-        out_ref[s, 1] = gram(left, right)
-        out_ref[s, 2] = gram(right, right)
-
-
-def partial_integral(factors):
+        left, right = whole_ref[s, :, :LANES], whole_ref[s, :, LANES:]
+        second = gram(right, right)
+        out_ref[s, :LANES] = gram(left, right)
+        out_ref[s, LANES : 2 * LANES] = jnp.where(row <= col, gram(left, left), second)
+        diagonal = jnp.sum(jnp.where(row == col, second, 0.0), axis=0, keepdims=True)
+        out_ref[s, 2 * LANES :] = jnp.broadcast_to(diagonal, (HALF, LANES))
+
+
+def partial_integral(whole):
     return pl.pallas_call(
         partial_kernel,
-        in_specs=[VMEM] * len(factors),
+        in_specs=[VMEM],
         out_specs=VMEM,
-        out_shape=jax.ShapeDtypeStruct((2, 3, LANES, LANES), jnp.float32),
+        out_shape=jax.ShapeDtypeStruct((2, 2 * LANES + HALF, LANES), jnp.float32),
         compiler_params=params(),
         cost_estimate=cost(2**27, 2**20),
         name="partial_integral",
-    )(*factors)
-
-
-def sigma_kernel(images_ref, *refs):
-    out_ref = refs[-1]
-    parts = refs[:-1]
+    )(whole)
+
+
+def sigma_kernel(images_ref, here_ref, there_ref, out_ref):
+    row = lax.broadcasted_iota(jnp.int32, (LANES, LANES), 0)
+    col = lax.broadcasted_iota(jnp.int32, (LANES, LANES), 1)
     for s in range(2):
-        total = parts[0][s]
-        for part in parts[1:]:
-            total = total + part[s]
-        total = total.astype(jnp.bfloat16)
+        total = here_ref[s] + there_ref[s]
+        mixed = total[:LANES].astype(jnp.bfloat16)
+        folded = total[LANES : 2 * LANES]
+        flipped = folded.T
+        top = jnp.where(row <= col, folded, flipped).astype(jnp.bfloat16)
+        low = jnp.where(row < col, flipped, folded)
+        low = jnp.where(row == col, jnp.broadcast_to(total[2 * LANES : 2 * LANES + 1], low.shape), low)
+        low = low.astype(jnp.bfloat16)
         green = []
         for jh in range(2):
             tiles = []
             for t in range(TAU):
                 for ih in range(2):
-                    tile = images_ref[(t * 2 + ih) * 2 + jh].astype(jnp.float32)
+                    tile = images_ref[CAME[(t * 2 + ih) * 2 + jh]].astype(jnp.float32)
                     tiles.append(tile[s * HALF : (s + 1) * HALF])
             green.append(tiles)
         first, second = (jnp.concatenate(tiles, axis=0).astype(jnp.bfloat16) for tiles in green)
         left = (
-            jnp.dot(first, total[0], preferred_element_type=jnp.float32)
-            + lax.dot_general(second, total[1], (((1,), (1,)), ((), ())), preferred_element_type=jnp.float32),
-            jnp.dot(first, total[1], preferred_element_type=jnp.float32)
-            + jnp.dot(second, total[2], preferred_element_type=jnp.float32),
+            jnp.dot(first, top, preferred_element_type=jnp.float32)
+            + lax.dot_general(second, mixed, (((1,), (1,)), ((), ())), preferred_element_type=jnp.float32),
+            jnp.dot(first, mixed, preferred_element_type=jnp.float32)
+            + jnp.dot(second, low, preferred_element_type=jnp.float32),
         )
         for jh in range(2):
             for t in range(TAU):
@@ -193,16 +201,16 @@
                     )
 
 
-def self_energy(images, parts):
+def self_energy(images, here, there):
     return pl.pallas_call(
         sigma_kernel,
-        in_specs=[VMEM] * (1 + len(parts)),
+        in_specs=[VMEM] * 3,
         out_specs=VMEM,
         out_shape=jax.ShapeDtypeStruct((2, TAU, 2 * HALF, 2 * LANES), jnp.float32),
         compiler_params=params(),
         cost_estimate=cost(2**26, 2**20),
         name="self_energy",
-    )(images, *parts)
+    )(images, here, there)
 
 
 def lines():
@@ -230,11 +238,11 @@
 def per_device(green_k, band_of_image, fit_tensor):
     packed, factor = pack(green_k, band_of_image, fit_tensor)
     block = lax.all_to_all(packed, "img", 0, 0, tiled=True, axis_index_groups=[ORDER])
-    part = partial_integral([lax.all_gather(factor, ("img", "orb"), axis=1, tiled=True, axis_index_groups=lines())])
+    part = partial_integral(lax.all_gather(factor, ("img", "orb"), axis=1, tiled=True, axis_index_groups=lines()))
     pair = part + exchanged(part, lambda at: at ^ 1, 1)
     other = exchanged(pair, lambda at: at + 1 if at % 2 else at - 1, 1)
-    images = lax.all_to_all(transform(block), "img", 0, 0, tiled=True, axis_index_groups=[ORDER])
-    return self_energy(images, [pair, other])
+    images = lax.all_to_all(transform(block), "img", 0, 0, tiled=True, axis_index_groups=[BACK_ORDER])
+    return self_energy(images, pair, other)
 
 
 def solution(mesh):

time: 61.4 us -> 59.7 us (0.972)
  starting transfers between devices: 39 us -> 36.9 us
    all_to_all x1, starting transfers between devices: 14.4 us -> 12.7 us  [per_device(): lax.all_to_all(transform(block), 'img', 0, 0, tiled=True, axis_index_grou...]
    all_to_all x1, waiting for transfers between devices: 0.01 us -> 1.62 us  [per_device(): lax.all_to_all(packed, 'img', 0, 0, tiled=True, axis_index_groups=[ORDER])]
    ppermute x2, waiting for transfers between devices: 5.98 us -> 4.67 us  [exchanged(): return lax.ppermute(value, ('img', 'orb'), pairs)]
  transfers between devices with their start and end apart: 4 -> 4, of which waited for: 1 -> 2; matrix products, arithmetic and copies ran while one was open for 0% -> 0% of each run, Pallas kernels for 2% -> 2%
where the time goes in v3:
time: 59.7 us; the launch traced here: 59.4 us
  starting transfers between devices  36.9 us (62%)
  blocking collectives  11.5 us (19%)
  waiting for transfers between devices  6.29 us (11%)
  Pallas kernels  4.56 us (8%)
    all_to_all x1, starting transfers between devices, per_device(): lax.all_to_all(packed, 'img', 0, 0, tiled=True, axis_index_groups=[ORDER])  17 us
    all_to_all x1, starting transfers between devices, per_device(): lax.all_to_all(transform(block), 'img', 0, 0, tiled=True, axis_index_grou...  12.7 us
    all_gather x1, blocking collectives, per_device(): lax.all_gather(factor, ('img', 'orb'), axis=1, tiled=True, axis_index_gro...  11.5 us
    ppermute x2, starting transfers between devices, exchanged(): return lax.ppermute(value, ('img', 'orb'), pairs)  7.15 us
    ppermute x2, waiting for transfers between devices, exchanged(): return lax.ppermute(value, ('img', 'orb'), pairs)  4.67 us
    pallas_call x1, Pallas kernels, pack(): pl.pallas_call(pack_kernel, in_specs=[HBM] * 3, out_specs=[VMEM] * 2, out...  2.34 us
    all_to_all x1, waiting for transfers between devices, per_device(): lax.all_to_all(packed, 'img', 0, 0, tiled=True, axis_index_groups=[ORDER])  1.62 us
  transfers between devices with their start and end apart: 4, of which 2 were waited for; matrix products, arithmetic and copies ran while one was open for 0% of the time, Pallas kernels for 2%

profile of v3, /device:TPU:1, one launch (start us, length us, event | category | flops | bytes accessed | tf_op | source)
XLA Modules:
  0.0 59.4 jit_solution(10537942311903498928)
XLA Ops:
  0.0 2.3 %pack.1 = (bf16[32,32,128]{2,1,0:T(8,128)(2,1)}, bf16[2,128,256]{2,1,0:T(8,128)(2,1)}) custom-call(s32[2]{0:T(128)} %band_hbm.1, f32[2,8,2,16,256]{4,3,2,1,0:T(8,128)} %green_hbm.1, bf16[32,128,256]{2,1,0:T(8,128)(2,1)} %fit_hbm.1), custom_call_target="tpu_custom_call" | custom-call | flops 262144 | bytes 1048576 | tf_op jit(solution)/shard_map/pack/pallas_call | solution.py:59
  2.3 17.0 %all-to-all-start = ((bf16[32,32,128]{2,1,0:T(8,128)(2,1)}), bf16[32,32,128]{2,1,0:T(8,128)(2,1)S(1)}, u32[]{:S(2)}, u32[]{:S(2)}) async-start(bf16[32,32,128]{2,1,0:T(8,128)(2,1)} %get-tuple-element.7), calls=%async_computation | async-start | bytes 524288 | tf_op jit(solution)/shard_map/all_to_all | solution.py:240
  19.4 11.5 %all_gather.3.whole_ref = bf16[2,512,256]{2,1,0:T(8,128)(2,1)S(1)} all-gather(bf16[2,128,256]{2,1,0:T(8,128)(2,1)} %get-tuple-element.8), channel_id=1, replica_groups={{0,1,2,3},{4,5,6,7},{8,9,10,11},{12,13,14,15},{16,20,24,28},{17,21,25,2..., dimensions={1}, use_global_device_ids=true | all-gather | bytes 655360 | tf_op jit(solution)/shard_map/all_gather | solution.py:241
  30.9 0.4 partial_integral.1
  31.3 3.1 %collective-permute-start = (f32[2,264,128]{2,1,0:T(8,128)S(1)}, f32[2,264,128]{2,1,0:T(8,128)S(1)}, u32[]{:S(2)}, u32[]{:S(2)}) collective-permute-start(f32[2,264,128]{2,1,0:T(8,128)S(1)} %partial_integral.1), channel_id=1, source_target_pairs={{0,4},{1,5},{2,6},{3,7},{4,0},{5,1},{6,2},{7,3},{8,12},{9,13},{10,... | collective-permute-start | bytes 811016 | tf_op jit(solution)/shard_map/ppermute | solution.py:235
  34.4 1.6 %all-to-all-done.x_ref = bf16[32,32,128]{2,1,0:T(8,128)(2,1)S(1)} async-done(((bf16[32,32,128]{2,1,0:T(8,128)(2,1)}), bf16[32,32,128]{2,1,0:T(8,128)(2,1)S(1)}, u32[]{:S(2)}, u32[]{:S(2)}) %all-to-all-start) | async-done | bytes 262176 | tf_op jit(solution)/shard_map/all_to_all | solution.py:240
  36.0 0.8 %transform.1 = bf16[32,16,128]{2,1,0:T(8,128)(2,1)} custom-call(bf16[32,32,128]{2,1,0:T(8,128)(2,1)S(1)} %all-to-all-done.x_ref), custom_call_target="tpu_custom_call" | custom-call | flops 1048576 | bytes 1048576 | tf_op jit(solution)/shard_map/transform/pallas_call | solution.py:127
  36.8 12.7 %all-to-all-start.1 = ((bf16[32,16,128]{2,1,0:T(8,128)(2,1)}), bf16[32,16,128]{2,1,0:T(8,128)(2,1)S(1)}, u32[]{:S(2)}, u32[]{:S(2)}) async-start(bf16[32,16,128]{2,1,0:T(8,128)(2,1)} %transform.1), calls=%async_computation.1 | async-start | bytes 262144 | tf_op jit(solution)/shard_map/all_to_all | solution.py:244
  49.6 0.0 collective-permute-done
  49.6 4.0 %collective-permute-start.1 = (f32[2,264,128]{2,1,0:T(8,128)S(1)}, f32[2,264,128]{2,1,0:T(8,128)S(1)}, u32[]{:S(2)}, u32[]{:S(2)}) collective-permute-start(f32[2,264,128]{2,1,0:T(8,128)S(1)} %add.3.here_ref), channel_id=1, source_target_pairs={{0,12},{1,13},{2,14},{3,15},{4,8},{5,9},{6,10},{7,11},{8,4},{9,5},... | collective-permute-start | bytes 811016 | tf_op jit(solution)/shard_map/ppermute | solution.py:235
  53.7 4.7 %collective-permute-done.1.there_ref = f32[2,264,128]{2,1,0:T(8,128)S(1)} collective-permute-done((f32[2,264,128]{2,1,0:T(8,128)S(1)}, f32[2,264,128]{2,1,0:T(8,128)S(1)}, u32[]{:S(2)}, u32[]{:S(2)}) %collective-permute-start.1) | collective-permute-done | bytes 270368 | tf_op jit(solution)/shard_map/ppermute | solution.py:235
  58.3 0.0 all-to-all-done.1.images_ref
  58.3 1.0 %self_energy.1 = f32[2,8,16,256]{3,2,1,0:T(8,128)} custom-call(bf16[32,16,128]{2,1,0:T(8,128)(2,1)S(1)} %all-to-all-done.1.images_ref, f32[2,264,128]{2,1,0:T(8,128)S(1)} %add.3.here_ref, f32[2,264,128]{2,1,0:T(8,128)S(1)} %collective-permute-done.1.there_ref), custom_call_target="tpu_custom_call" | custom-call | flops 67108864 | bytes 1048576 | tf_op jit(solution)/shard_map/self_energy/pallas_call | solution.py:205
  (1 shorter events, 0.0 us)
Async XLA Ops:
  2.3 33.7 %all-to-all-start = ((bf16[32,32,128]{2,1,0:T(8,128)(2,1)}), bf16[32,32,128]{2,1,0:T(8,128)(2,1)S(1)}, u32[]{:S(2)}, u32[]{:S(2)}) async-start(bf16[32,32,128]{2,1,0:T(8,128)(2,1)} %get-tuple-element.7), calls=%async_computation | async-start | bytes 524288 | tf_op jit(solution)/shard_map/all_to_all | solution.py:240
  31.3 18.3 %collective-permute-start = (f32[2,264,128]{2,1,0:T(8,128)S(1)}, f32[2,264,128]{2,1,0:T(8,128)S(1)}, u32[]{:S(2)}, u32[]{:S(2)}) collective-permute-start(f32[2,264,128]{2,1,0:T(8,128)S(1)} %partial_integral.1), channel_id=1, source_target_pairs={{0,4},{1,5},{2,6},{3,7},{4,0},{5,1},{6,2},{7,3},{8,12},{9,13},{10,... | collective-permute-start | bytes 811016 | tf_op jit(solution)/shard_map/ppermute | solution.py:235
  36.8 21.5 %all-to-all-start.1 = ((bf16[32,16,128]{2,1,0:T(8,128)(2,1)}), bf16[32,16,128]{2,1,0:T(8,128)(2,1)S(1)}, u32[]{:S(2)}, u32[]{:S(2)}) async-start(bf16[32,16,128]{2,1,0:T(8,128)(2,1)} %transform.1), calls=%async_computation.1 | async-start | bytes 262144 | tf_op jit(solution)/shard_map/all_to_all | solution.py:244
  49.6 8.7 %collective-permute-start.1 = (f32[2,264,128]{2,1,0:T(8,128)S(1)}, f32[2,264,128]{2,1,0:T(8,128)S(1)}, u32[]{:S(2)}, u32[]{:S(2)}) collective-permute-start(f32[2,264,128]{2,1,0:T(8,128)S(1)} %add.3.here_ref), channel_id=1, source_target_pairs={{0,12},{1,13},{2,14},{3,15},{4,8},{5,9},{6,10},{7,11},{8,4},{9,5},... | collective-permute-start | bytes 811016 | tf_op jit(solution)/shard_map/ppermute | solution.py:235

commit v4 on v3

--- a/solution.py
+++ b/solution.py
@@ -31,16 +31,15 @@
     points = green.shape[0]
     bands = pltpu.make_async_copy(band_hbm, band, sems.at[2 * points])
     bands.start()
-    loads = [pltpu.make_async_copy(green_hbm.at[p], green.at[p], sems.at[p]) for p in range(points)]
-    for load in loads:
-        load.start()
+    load = pltpu.make_async_copy(green_hbm, green, sems.at[0])
+    load.start()
     bands.wait()
     fits = []
     for p in range(points):
         fits.append(pltpu.make_async_copy(fit_hbm.at[band[p]], factor_ref.at[p], sems.at[points + p]))
         fits[p].start()
+    load.wait()
     for p in range(points):
-        loads[p].wait()
         for t in range(TAU):
             for ih in range(2):
                 rows = slice(ih * HALF, (ih + 1) * HALF)
@@ -170,6 +169,7 @@
     for s in range(2):
         total = here_ref[s] + there_ref[s]
         mixed = total[:LANES].astype(jnp.bfloat16)
+        turned = total[:LANES].T.astype(jnp.bfloat16)
         folded = total[LANES : 2 * LANES]
         flipped = folded.T
         top = jnp.where(row <= col, folded, flipped).astype(jnp.bfloat16)
@@ -185,12 +185,11 @@
                     tiles.append(tile[s * HALF : (s + 1) * HALF])
             green.append(tiles)
         first, second = (jnp.concatenate(tiles, axis=0).astype(jnp.bfloat16) for tiles in green)
-        left = (
-            jnp.dot(first, top, preferred_element_type=jnp.float32)
-            + lax.dot_general(second, mixed, (((1,), (1,)), ((), ())), preferred_element_type=jnp.float32),
-            jnp.dot(first, mixed, preferred_element_type=jnp.float32)
-            + jnp.dot(second, low, preferred_element_type=jnp.float32),
+        whole = jnp.concatenate(
+            [jnp.concatenate([top, mixed], axis=1), jnp.concatenate([turned, low], axis=1)], axis=0
         )
+        product = jnp.dot(jnp.concatenate([first, second], axis=1), whole, preferred_element_type=jnp.float32)
+        left = (product[:, :LANES], product[:, LANES:])
         for jh in range(2):
             for t in range(TAU):
                 for ih in range(2):

time: 59.7 us -> 59.7 us (level)
  no operation moved by 1% of the time
where the time goes in v4:
time: 59.7 us; the launch traced here: 59.3 us
  starting transfers between devices  36.9 us (62%)
  blocking collectives  11.5 us (19%)
  waiting for transfers between devices  6.29 us (11%)
  Pallas kernels  4.53 us (8%)
    all_to_all x1, starting transfers between devices, per_device(): lax.all_to_all(packed, 'img', 0, 0, tiled=True, axis_index_groups=[ORDER])  17 us
    all_to_all x1, starting transfers between devices, per_device(): lax.all_to_all(transform(block), 'img', 0, 0, tiled=True, axis_index_grou...  12.7 us
    all_gather x1, blocking collectives, per_device(): lax.all_gather(factor, ('img', 'orb'), axis=1, tiled=True, axis_index_gro...  11.5 us
    ppermute x2, starting transfers between devices, exchanged(): return lax.ppermute(value, ('img', 'orb'), pairs)  7.15 us
    ppermute x2, waiting for transfers between devices, exchanged(): return lax.ppermute(value, ('img', 'orb'), pairs)  4.67 us
    pallas_call x1, Pallas kernels, pack(): pl.pallas_call(pack_kernel, in_specs=[HBM] * 3, out_specs=[VMEM] * 2, out...  2.34 us
    all_to_all x1, waiting for transfers between devices, per_device(): lax.all_to_all(packed, 'img', 0, 0, tiled=True, axis_index_groups=[ORDER])  1.62 us
  transfers between devices with their start and end apart: 4, of which 2 were waited for; matrix products, arithmetic and copies ran while one was open for 0% of the time, Pallas kernels for 2%

profile of v4, /device:TPU:1, one launch (start us, length us, event | category | flops | bytes accessed | tf_op | source)
XLA Modules:
  0.0 59.3 jit_solution(9640861317172804710)
XLA Ops:
  0.0 2.3 %pack.1 = (bf16[32,32,128]{2,1,0:T(8,128)(2,1)}, bf16[2,128,256]{2,1,0:T(8,128)(2,1)}) custom-call(s32[2]{0:T(128)} %band_hbm.1, f32[2,8,2,16,256]{4,3,2,1,0:T(8,128)} %green_hbm.1, bf16[32,128,256]{2,1,0:T(8,128)(2,1)} %fit_hbm.1), custom_call_target="tpu_custom_call" | custom-call | flops 262144 | bytes 1048576 | tf_op jit(solution)/shard_map/pack/pallas_call | solution.py:58
  2.3 17.0 %all-to-all-start = ((bf16[32,32,128]{2,1,0:T(8,128)(2,1)}), bf16[32,32,128]{2,1,0:T(8,128)(2,1)S(1)}, u32[]{:S(2)}, u32[]{:S(2)}) async-start(bf16[32,32,128]{2,1,0:T(8,128)(2,1)} %get-tuple-element.7), calls=%async_computation | async-start | bytes 524288 | tf_op jit(solution)/shard_map/all_to_all | solution.py:239
  19.4 11.5 %all_gather.3.whole_ref = bf16[2,512,256]{2,1,0:T(8,128)(2,1)S(1)} all-gather(bf16[2,128,256]{2,1,0:T(8,128)(2,1)} %get-tuple-element.8), channel_id=1, replica_groups={{0,1,2,3},{4,5,6,7},{8,9,10,11},{12,13,14,15},{16,20,24,28},{17,21,25,2..., dimensions={1}, use_global_device_ids=true | all-gather | bytes 655360 | tf_op jit(solution)/shard_map/all_gather | solution.py:240
  30.9 0.4 partial_integral.1
  31.3 3.1 %collective-permute-start = (f32[2,264,128]{2,1,0:T(8,128)S(1)}, f32[2,264,128]{2,1,0:T(8,128)S(1)}, u32[]{:S(2)}, u32[]{:S(2)}) collective-permute-start(f32[2,264,128]{2,1,0:T(8,128)S(1)} %partial_integral.1), channel_id=1, source_target_pairs={{0,4},{1,5},{2,6},{3,7},{4,0},{5,1},{6,2},{7,3},{8,12},{9,13},{10,... | collective-permute-start | bytes 811016 | tf_op jit(solution)/shard_map/ppermute | solution.py:234
  34.4 1.6 %all-to-all-done.x_ref = bf16[32,32,128]{2,1,0:T(8,128)(2,1)S(1)} async-done(((bf16[32,32,128]{2,1,0:T(8,128)(2,1)}), bf16[32,32,128]{2,1,0:T(8,128)(2,1)S(1)}, u32[]{:S(2)}, u32[]{:S(2)}) %all-to-all-start) | async-done | bytes 262176 | tf_op jit(solution)/shard_map/all_to_all | solution.py:239
  36.0 0.8 %transform.1 = bf16[32,16,128]{2,1,0:T(8,128)(2,1)} custom-call(bf16[32,32,128]{2,1,0:T(8,128)(2,1)S(1)} %all-to-all-done.x_ref), custom_call_target="tpu_custom_call" | custom-call | flops 1048576 | bytes 1048576 | tf_op jit(solution)/shard_map/transform/pallas_call | solution.py:126
  36.8 12.7 %all-to-all-start.1 = ((bf16[32,16,128]{2,1,0:T(8,128)(2,1)}), bf16[32,16,128]{2,1,0:T(8,128)(2,1)S(1)}, u32[]{:S(2)}, u32[]{:S(2)}) async-start(bf16[32,16,128]{2,1,0:T(8,128)(2,1)} %transform.1), calls=%async_computation.1 | async-start | bytes 262144 | tf_op jit(solution)/shard_map/all_to_all | solution.py:243
  49.6 0.0 collective-permute-done
  49.6 4.0 %collective-permute-start.1 = (f32[2,264,128]{2,1,0:T(8,128)S(1)}, f32[2,264,128]{2,1,0:T(8,128)S(1)}, u32[]{:S(2)}, u32[]{:S(2)}) collective-permute-start(f32[2,264,128]{2,1,0:T(8,128)S(1)} %add.3.here_ref), channel_id=1, source_target_pairs={{0,12},{1,13},{2,14},{3,15},{4,8},{5,9},{6,10},{7,11},{8,4},{9,5},... | collective-permute-start | bytes 811016 | tf_op jit(solution)/shard_map/ppermute | solution.py:234
  53.7 4.7 %collective-permute-done.1.there_ref = f32[2,264,128]{2,1,0:T(8,128)S(1)} collective-permute-done((f32[2,264,128]{2,1,0:T(8,128)S(1)}, f32[2,264,128]{2,1,0:T(8,128)S(1)}, u32[]{:S(2)}, u32[]{:S(2)}) %collective-permute-start.1) | collective-permute-done | bytes 270368 | tf_op jit(solution)/shard_map/ppermute | solution.py:234
  58.3 0.0 all-to-all-done.1.images_ref
  58.3 1.0 %self_energy.1 = f32[2,8,16,256]{3,2,1,0:T(8,128)} custom-call(bf16[32,16,128]{2,1,0:T(8,128)(2,1)S(1)} %all-to-all-done.1.images_ref, f32[2,264,128]{2,1,0:T(8,128)S(1)} %add.3.here_ref, f32[2,264,128]{2,1,0:T(8,128)S(1)} %collective-permute-done.1.there_ref), custom_call_target="tpu_custom_call" | custom-call | flops 67108864 | bytes 1048576 | tf_op jit(solution)/shard_map/self_energy/pallas_call | solution.py:204
  (1 shorter events, 0.0 us)
Async XLA Ops:
  2.3 33.7 %all-to-all-start = ((bf16[32,32,128]{2,1,0:T(8,128)(2,1)}), bf16[32,32,128]{2,1,0:T(8,128)(2,1)S(1)}, u32[]{:S(2)}, u32[]{:S(2)}) async-start(bf16[32,32,128]{2,1,0:T(8,128)(2,1)} %get-tuple-element.7), calls=%async_computation | async-start | bytes 524288 | tf_op jit(solution)/shard_map/all_to_all | solution.py:239
  31.3 18.3 %collective-permute-start = (f32[2,264,128]{2,1,0:T(8,128)S(1)}, f32[2,264,128]{2,1,0:T(8,128)S(1)}, u32[]{:S(2)}, u32[]{:S(2)}) collective-permute-start(f32[2,264,128]{2,1,0:T(8,128)S(1)} %partial_integral.1), channel_id=1, source_target_pairs={{0,4},{1,5},{2,6},{3,7},{4,0},{5,1},{6,2},{7,3},{8,12},{9,13},{10,... | collective-permute-start | bytes 811016 | tf_op jit(solution)/shard_map/ppermute | solution.py:234
  36.8 21.5 %all-to-all-start.1 = ((bf16[32,16,128]{2,1,0:T(8,128)(2,1)}), bf16[32,16,128]{2,1,0:T(8,128)(2,1)S(1)}, u32[]{:S(2)}, u32[]{:S(2)}) async-start(bf16[32,16,128]{2,1,0:T(8,128)(2,1)} %transform.1), calls=%async_computation.1 | async-start | bytes 262144 | tf_op jit(solution)/shard_map/all_to_all | solution.py:243
  49.6 8.7 %collective-permute-start.1 = (f32[2,264,128]{2,1,0:T(8,128)S(1)}, f32[2,264,128]{2,1,0:T(8,128)S(1)}, u32[]{:S(2)}, u32[]{:S(2)}) collective-permute-start(f32[2,264,128]{2,1,0:T(8,128)S(1)} %add.3.here_ref), channel_id=1, source_target_pairs={{0,12},{1,13},{2,14},{3,15},{4,8},{5,9},{6,10},{7,11},{8,4},{9,5},... | collective-permute-start | bytes 811016 | tf_op jit(solution)/shard_map/ppermute | solution.py:234

commit v5 on v4

--- a/solution.py
+++ b/solution.py
@@ -12,7 +12,7 @@
 VMEM = pl.BlockSpec(memory_space=pltpu.VMEM)
 HBM = pl.BlockSpec(memory_space=pltpu.HBM)
 ORDER = [24, 22, 20, 18, 16, 14, 12, 10, 8, 6, 4, 2, 0, 30, 28, 26, 25, 23, 21, 19, 17, 15, 13, 11, 9, 7, 5, 3, 1, 31, 29, 27]
-BACK_ORDER = [20, 18, 16, 14, 12, 10, 8, 6, 4, 2, 0, 30, 28, 26, 24, 22, 21, 19, 17, 15, 13, 11, 9, 7, 5, 3, 1, 31, 29, 27, 25, 23]
+BACK_ORDER = [18, 19, 16, 17, 14, 15, 12, 13, 10, 11, 8, 9, 6, 7, 4, 5, 2, 3, 0, 1, 30, 31, 28, 29, 26, 27, 24, 25, 22, 23, 20, 21]
 PLACE = [ORDER.index(img) for img in range(32)]
 BACK_PLACE = [BACK_ORDER.index(img) for img in range(32)]
 CAME = [BACK_PLACE[img] for img in ORDER]

time: 59.7 us -> 59.7 us (level)
  no operation moved by 1% of the time
where the time goes in v5:
time: 59.7 us; the launch traced here: 59.3 us
  starting transfers between devices  36.9 us (62%)
  blocking collectives  11.5 us (19%)
  waiting for transfers between devices  6.3 us (11%)
  Pallas kernels  4.53 us (8%)
    all_to_all x1, starting transfers between devices, per_device(): lax.all_to_all(packed, 'img', 0, 0, tiled=True, axis_index_groups=[ORDER])  17 us
    all_to_all x1, starting transfers between devices, per_device(): lax.all_to_all(transform(block), 'img', 0, 0, tiled=True, axis_index_grou...  12.7 us
    all_gather x1, blocking collectives, per_device(): lax.all_gather(factor, ('img', 'orb'), axis=1, tiled=True, axis_index_gro...  11.5 us
    ppermute x2, starting transfers between devices, exchanged(): return lax.ppermute(value, ('img', 'orb'), pairs)  7.15 us
    ppermute x2, waiting for transfers between devices, exchanged(): return lax.ppermute(value, ('img', 'orb'), pairs)  4.67 us
    pallas_call x1, Pallas kernels, pack(): pl.pallas_call(pack_kernel, in_specs=[HBM] * 3, out_specs=[VMEM] * 2, out...  2.34 us
    all_to_all x1, waiting for transfers between devices, per_device(): lax.all_to_all(packed, 'img', 0, 0, tiled=True, axis_index_groups=[ORDER])  1.62 us
  transfers between devices with their start and end apart: 4, of which 2 were waited for; matrix products, arithmetic and copies ran while one was open for 0% of the time, Pallas kernels for 2%

profile of v5, /device:TPU:1, one launch (start us, length us, event | category | flops | bytes accessed | tf_op | source)
XLA Modules:
  0.0 59.3 jit_solution(9533322592718989504)
XLA Ops:
  0.0 2.3 %pack.1 = (bf16[32,32,128]{2,1,0:T(8,128)(2,1)}, bf16[2,128,256]{2,1,0:T(8,128)(2,1)}) custom-call(s32[2]{0:T(128)} %band_hbm.1, f32[2,8,2,16,256]{4,3,2,1,0:T(8,128)} %green_hbm.1, bf16[32,128,256]{2,1,0:T(8,128)(2,1)} %fit_hbm.1), custom_call_target="tpu_custom_call" | custom-call | flops 262144 | bytes 1048576 | tf_op jit(solution)/shard_map/pack/pallas_call | solution.py:58
  2.3 17.0 %all-to-all-start = ((bf16[32,32,128]{2,1,0:T(8,128)(2,1)}), bf16[32,32,128]{2,1,0:T(8,128)(2,1)S(1)}, u32[]{:S(2)}, u32[]{:S(2)}) async-start(bf16[32,32,128]{2,1,0:T(8,128)(2,1)} %get-tuple-element.7), calls=%async_computation | async-start | bytes 524288 | tf_op jit(solution)/shard_map/all_to_all | solution.py:239
  19.4 11.5 %all_gather.3.whole_ref = bf16[2,512,256]{2,1,0:T(8,128)(2,1)S(1)} all-gather(bf16[2,128,256]{2,1,0:T(8,128)(2,1)} %get-tuple-element.8), channel_id=1, replica_groups={{0,1,2,3},{4,5,6,7},{8,9,10,11},{12,13,14,15},{16,20,24,28},{17,21,25,2..., dimensions={1}, use_global_device_ids=true | all-gather | bytes 655360 | tf_op jit(solution)/shard_map/all_gather | solution.py:240
  30.9 0.4 partial_integral.1
  31.3 3.1 %collective-permute-start = (f32[2,264,128]{2,1,0:T(8,128)S(1)}, f32[2,264,128]{2,1,0:T(8,128)S(1)}, u32[]{:S(2)}, u32[]{:S(2)}) collective-permute-start(f32[2,264,128]{2,1,0:T(8,128)S(1)} %partial_integral.1), channel_id=1, source_target_pairs={{0,4},{1,5},{2,6},{3,7},{4,0},{5,1},{6,2},{7,3},{8,12},{9,13},{10,... | collective-permute-start | bytes 811016 | tf_op jit(solution)/shard_map/ppermute | solution.py:234
  34.4 1.6 %all-to-all-done.x_ref = bf16[32,32,128]{2,1,0:T(8,128)(2,1)S(1)} async-done(((bf16[32,32,128]{2,1,0:T(8,128)(2,1)}), bf16[32,32,128]{2,1,0:T(8,128)(2,1)S(1)}, u32[]{:S(2)}, u32[]{:S(2)}) %all-to-all-start) | async-done | bytes 262176 | tf_op jit(solution)/shard_map/all_to_all | solution.py:239
  36.0 0.8 %transform.1 = bf16[32,16,128]{2,1,0:T(8,128)(2,1)} custom-call(bf16[32,32,128]{2,1,0:T(8,128)(2,1)S(1)} %all-to-all-done.x_ref), custom_call_target="tpu_custom_call" | custom-call | flops 1048576 | bytes 1048576 | tf_op jit(solution)/shard_map/transform/pallas_call | solution.py:126
  36.8 12.7 %all-to-all-start.1 = ((bf16[32,16,128]{2,1,0:T(8,128)(2,1)}), bf16[32,16,128]{2,1,0:T(8,128)(2,1)S(1)}, u32[]{:S(2)}, u32[]{:S(2)}) async-start(bf16[32,16,128]{2,1,0:T(8,128)(2,1)} %transform.1), calls=%async_computation.1 | async-start | bytes 262144 | tf_op jit(solution)/shard_map/all_to_all | solution.py:243
  49.6 0.0 collective-permute-done
  49.6 4.0 %collective-permute-start.1 = (f32[2,264,128]{2,1,0:T(8,128)S(1)}, f32[2,264,128]{2,1,0:T(8,128)S(1)}, u32[]{:S(2)}, u32[]{:S(2)}) collective-permute-start(f32[2,264,128]{2,1,0:T(8,128)S(1)} %add.3.here_ref), channel_id=1, source_target_pairs={{0,12},{1,13},{2,14},{3,15},{4,8},{5,9},{6,10},{7,11},{8,4},{9,5},... | collective-permute-start | bytes 811016 | tf_op jit(solution)/shard_map/ppermute | solution.py:234
  53.7 4.7 %collective-permute-done.1.there_ref = f32[2,264,128]{2,1,0:T(8,128)S(1)} collective-permute-done((f32[2,264,128]{2,1,0:T(8,128)S(1)}, f32[2,264,128]{2,1,0:T(8,128)S(1)}, u32[]{:S(2)}, u32[]{:S(2)}) %collective-permute-start.1) | collective-permute-done | bytes 270368 | tf_op jit(solution)/shard_map/ppermute | solution.py:234
  58.3 0.0 all-to-all-done.1.images_ref
  58.3 1.0 %self_energy.1 = f32[2,8,16,256]{3,2,1,0:T(8,128)} custom-call(bf16[32,16,128]{2,1,0:T(8,128)(2,1)S(1)} %all-to-all-done.1.images_ref, f32[2,264,128]{2,1,0:T(8,128)S(1)} %add.3.here_ref, f32[2,264,128]{2,1,0:T(8,128)S(1)} %collective-permute-done.1.there_ref), custom_call_target="tpu_custom_call" | custom-call | flops 67108864 | bytes 1048576 | tf_op jit(solution)/shard_map/self_energy/pallas_call | solution.py:204
  (1 shorter events, 0.0 us)
Async XLA Ops:
  2.3 33.7 %all-to-all-start = ((bf16[32,32,128]{2,1,0:T(8,128)(2,1)}), bf16[32,32,128]{2,1,0:T(8,128)(2,1)S(1)}, u32[]{:S(2)}, u32[]{:S(2)}) async-start(bf16[32,32,128]{2,1,0:T(8,128)(2,1)} %get-tuple-element.7), calls=%async_computation | async-start | bytes 524288 | tf_op jit(solution)/shard_map/all_to_all | solution.py:239
  31.3 18.3 %collective-permute-start = (f32[2,264,128]{2,1,0:T(8,128)S(1)}, f32[2,264,128]{2,1,0:T(8,128)S(1)}, u32[]{:S(2)}, u32[]{:S(2)}) collective-permute-start(f32[2,264,128]{2,1,0:T(8,128)S(1)} %partial_integral.1), channel_id=1, source_target_pairs={{0,4},{1,5},{2,6},{3,7},{4,0},{5,1},{6,2},{7,3},{8,12},{9,13},{10,... | collective-permute-start | bytes 811016 | tf_op jit(solution)/shard_map/ppermute | solution.py:234
  36.8 21.5 %all-to-all-start.1 = ((bf16[32,16,128]{2,1,0:T(8,128)(2,1)}), bf16[32,16,128]{2,1,0:T(8,128)(2,1)S(1)}, u32[]{:S(2)}, u32[]{:S(2)}) async-start(bf16[32,16,128]{2,1,0:T(8,128)(2,1)} %transform.1), calls=%async_computation.1 | async-start | bytes 262144 | tf_op jit(solution)/shard_map/all_to_all | solution.py:243
  49.6 8.7 %collective-permute-start.1 = (f32[2,264,128]{2,1,0:T(8,128)S(1)}, f32[2,264,128]{2,1,0:T(8,128)S(1)}, u32[]{:S(2)}, u32[]{:S(2)}) collective-permute-start(f32[2,264,128]{2,1,0:T(8,128)S(1)} %add.3.here_ref), channel_id=1, source_target_pairs={{0,12},{1,13},{2,14},{3,15},{4,8},{5,9},{6,10},{7,11},{8,4},{9,5},... | collective-permute-start | bytes 811016 | tf_op jit(solution)/shard_map/ppermute | solution.py:234
